TPU v7x, 512 devices: a whole 4x8x8 slice. The times are simulated.
512 devices in a mesh: row: 16 (over z_lo, x), col: 32 (over y, z_hi, core).
Axes of the slice: x: 4, y: 8, z: 8 (z_hi: 2, z_lo: 4; z = z_hi * 4 + z_lo), core: 2. Of those that a mesh axis runs over, the one named last changes fastest.
Arguments:
- positions: float32 [3, 32768], P(None, ('row', 'col')), may hold values from -1 to 1
- orient: float32 [2, 32768], P(None, ('row', 'col')), may hold values from -3.140625 to 3.140625
- areas: float32 [32768], P(('row', 'col')), may hold values from 0.008 to 0.16
- incident: float32 [2, 3, 2, 32768], P(None, None, None, ('row', 'col')), may hold values from -6 to 6
- visible: int32 [512, 16, 32], P('row', None, 'col'), may hold values 0 or 1
Outputs:
- currents: float32 [2, 3, 2, 32768], P(None, None, None, ('row', 'col'))
All inputs are finite; a program needn't handle non-finite values. No bound on the sum of `visible` on one device may be relied on, other than what follows from the above.
Results may differ from a plain program's by a relative error of at most 0.006.
Values may be sent and summed in bfloat16 or wider, within the bound.
A program may use at most 64 MiB of HBM per device.

v0:
```python
import math

import jax
import jax.numpy as jnp
from jax import lax
from jax.sharding import PartitionSpec as P

ITERS = 3


wave_number = 8.0 * math.pi
soft_square = 0.0025


def rows_first(arrays, axis, dims):
    turned = [jnp.moveaxis(a, dim, 0) for a, dim in zip(arrays, dims)]
    widths = [t[0].size for t in turned]
    both = jnp.concatenate([t.reshape(-1, w) for t, w in zip(turned, widths)], axis=1)
    whole = lax.all_gather(both, axis, axis=0, tiled=True)
    tiles = jnp.split(whole, [sum(widths[:k]) for k in range(1, len(widths))], axis=1)
    return tuple(
        (
            jnp.moveaxis(b.reshape(-1, *t.shape[1:]), 0, dim)
            for b, t, dim in zip(tiles, turned, dims)
        )
    )


def sent_to_all(shard, axis):
    copies = jnp.broadcast_to(shard, (lax.axis_size(axis), *shard.shape))
    return lax.all_to_all(copies, axis, split_axis=0, concat_axis=0, tiled=True)


def in_order(tiles, dim):
    tiles = jnp.moveaxis(tiles, 0, dim)
    lengths = tiles.shape
    return tiles.reshape(*lengths[:dim], lengths[dim] * lengths[dim + 1], *lengths[dim + 2 :])


def gathered_copies(shard, axis, dim):
    tiles = sent_to_all(shard, axis)
    return in_order(tiles, dim)


def cut_along(shard, dim, count):
    before, after = (shard.shape[:dim], shard.shape[dim + 1 :])
    return jnp.moveaxis(shard.reshape(*before, count, -1, *after), dim, 0)


def summed_on_arrival(shard, axis, dim):
    count = lax.axis_size(axis)
    tiles = lax.all_to_all(cut_along(shard, dim, count), axis, 0, 0, tiled=True)
    return jnp.sum(tiles, axis=0)


def normals_from(orient):
    polar_angle = orient[0]
    azimuth = orient[1]
    return jnp.stack(
        [
            jnp.sin(polar_angle) * jnp.cos(azimuth),
            jnp.sin(polar_angle) * jnp.sin(azimuth),
            jnp.cos(polar_angle),
        ]
    )


def right_operand(outgoing, position):
    moments = (position[None, :, None, None, :] * outgoing[:, None].astype(jnp.float32)).astype(
        jnp.bfloat16
    )
    stacked = jnp.concatenate([outgoing[:, None], moments], axis=1)
    flattened = stacked.reshape(2, -1, stacked.shape[-1])
    real_part = flattened[0]
    imag_part = flattened[1]
    upper = jnp.concatenate([real_part, -imag_part], axis=1)
    lower = jnp.concatenate([imag_part, real_part], axis=1)
    return jnp.concatenate([upper, lower], axis=0)


def twisted(products, position, normal):
    direct = products[:, 0]
    moments = products[:, 1:]
    normal_dot = jnp.sum(normal[None, :, None, :] * direct, axis=1)
    height = jnp.sum(normal * position, axis=0)
    twist_part = moments - jnp.swapaxes(moments, 1, 2)
    turned = jnp.sum(normal[None, None, :, None, :] * twist_part, axis=2)
    return position[None, :, None, :] * normal_dot[:, None] - height * direct - turned


def kernel_block(obs_position, visible_rows, src_position, src_weight, tiles_onehot):
    separation = obs_position[:, :, None] - src_position[:, None, :]
    dist_square = jnp.sum(separation * separation, axis=0) + soft_square
    distance = jnp.sqrt(dist_square)
    phase_arg = wave_number * distance
    visible_pairs = jnp.dot(visible_rows, tiles_onehot, preferred_element_type=jnp.float32)
    factor = visible_pairs * src_weight[None, :] / (dist_square * distance)
    cosine = jnp.cos(phase_arg)
    sine_part = jnp.sin(phase_arg)
    real_k = factor * (cosine + phase_arg * sine_part)
    imag_k = factor * (phase_arg * cosine - sine_part)
    return jnp.stack([real_k, imag_k]).astype(jnp.bfloat16)


def shards(positions, orient, areas, incident, visible):
    shard_len = positions.shape[1]
    row_count = lax.axis_size("row")
    col_count = lax.axis_size("col")
    facet_total = shard_len * row_count * col_count
    weight_scale = 1.0 / (4.0 * math.pi * math.sqrt(facet_total))
    obs_position, obs_orient = rows_first((positions, orient), "col", (1, 1))
    src_position, src_area = rows_first((positions, areas), "row", (1, 0))
    src_weight = src_area * weight_scale
    obs_normal = normals_from(obs_orient)
    observed = obs_position.shape[1]
    src_len = src_position.shape[1]
    block_len = min(512, observed)
    block_count = observed // block_len
    tile_rows = jnp.repeat(visible[:, :, 0].astype(jnp.float32), shard_len, axis=0)
    obs_blocks = obs_position.reshape(3, block_count, block_len).transpose(1, 0, 2)
    row_blocks = tile_rows.reshape(block_count, block_len, row_count)
    tile_index = jnp.arange(src_len, dtype=jnp.int32) // shard_len
    tiles_onehot = (jnp.arange(row_count, dtype=jnp.int32)[:, None] == tile_index[None, :]).astype(
        jnp.float32
    )

    def one_block(block_pair):
        return kernel_block(block_pair[0], block_pair[1], src_position, src_weight, tiles_onehot)

    kernel_all = lax.map(one_block, (obs_blocks, row_blocks))
    polar_count = incident.shape[2]
    row_total = 24 * polar_count
    current = incident
    for bounce in range(ITERS):
        outgoing = current.astype(jnp.bfloat16)
        shard_part = gathered_copies(outgoing, "row", 3)
        part_len = shard_part.shape[-1]
        operand = right_operand(shard_part, src_position)
        first = lax.dot_general(
            operand[:, :part_len],
            kernel_all[:, 0],
            (((1,), (2,)), ((), ())),
            preferred_element_type=jnp.float32,
        )
        second = lax.dot_general(
            operand[:, part_len:],
            kernel_all[:, 1],
            (((1,), (2,)), ((), ())),
            preferred_element_type=jnp.float32,
        )
        products = (first + second).reshape(row_total, observed)
        partial_value = twisted(
            products.reshape(2, 4, 3, polar_count, observed), obs_position, obs_normal
        ).reshape(-1, observed)
        own_rows = summed_on_arrival(partial_value, "col", 1)
        scattered = own_rows.reshape(2, 3, polar_count, shard_len)
        current = incident + 2.0 * scattered
    return current


def solution(mesh):
    in_specs = (
        P(None, ("row", "col")),
        P(None, ("row", "col")),
        P(("row", "col")),
        P(None, None, None, ("row", "col")),
        P("row", None, "col"),
    )
    out_specs = P(None, None, None, ("row", "col"))
    return jax.shard_map(shards, mesh=mesh, in_specs=in_specs, out_specs=out_specs, check_vma=False)
```

profile of v0, /device:TPU:1, one launch (start us, length us, event | category | flops | bytes accessed | tf_op | source)
XLA Modules:
  0.0 268.4 jit_solution(10470882375531055421)
XLA Ops:
  0.0 0.7 convert_element_type.68
  0.7 0.7 reshape.153
  1.4 10.4 %all-to-all-start = ((bf16[16,2,384]{2,1,0:T(2,128)(2,1)}), bf16[16,2,384]{2,1,0:T(2,128)(2,1)S(1)}, u32[]{:S(2)}, u32[]{:S(2)}) async-start(bf16[16,2,384]{2,1,0:T(2,128)(2,1)} %reshape.153), calls=%async_computation | async-start | bytes 49152 | tf_op jit(solution)/shard_map/all_to_all | solution.py:31
  11.8 0.7 maximum_bitcast_fusion.2
  12.5 35.2 %all-gather.1 = f32[16,64,4]{1,2,0:T(4,128)S(1)} all-gather(f32[1,64,4]{1,2,0:T(4,128)S(1)} %maximum_bitcast_fusion.2), channel_id=1, replica_groups=mesh['row'=16,'col'=32] {'row'}, dimensions={0}, use_global_device_ids=true | all-gather | bytes 17408 | tf_op jit(solution)/shard_map/all_gather | solution.py:19
  47.8 0.7 maximum_bitcast_fusion.1
  48.5 63.9 %all-gather = f32[32,64,5]{1,2,0:T(8,128)S(1)} all-gather(f32[1,64,5]{1,2,0:T(8,128)S(1)} %maximum_bitcast_fusion.1), channel_id=1, replica_groups=mesh['row'=16,'col'=32] {'col'}, dimensions={0}, use_global_device_ids=true | all-gather | bytes 42240 | tf_op jit(solution)/shard_map/all_gather | solution.py:19
  112.5 0.7 convert_element_type.72
  113.5 50.9 %while.11 = (s32[]{:T(128)}, bf16[4,2,512,1024]{3,2,0,1:T(8,128)(2,1)}, bf16[4,512,16]{1,0,2:T(4,128)(2,1)S(1)}, f32[1024]{0:T(1024)S(1)}, f32[4,3,512]{2,0,1:T(...) while((s32[]{:T(128)}, bf16[4,2,512,1024]{3,2,0,1:T(8,128)(2,1)}, ...), condition=%wide.region_2.3_spmd.clone, body=%wide.region_0.2_spmd.clone.sunk | while | flops 32014336 | bytes 10586217 | solution.py:130
  113.6 0.6 multiply_reduce_fusion.3
  114.3 10.5 %fusion.63 = (bf16[1,1,512,1024]{3,2,1,0:T(8,128)(2,1)S(1)}, bf16[1,1,512,1024]{3,2,1,0:T(8,128)(2,1)S(1)}) fusion(f32[512,1024]{1,0:T(8,128)S(1)} %multiply_reduce_fusion.3, f32[1024]{0:T(1024)S(1)} %get-tuple-element.194, s32[1024]{0:T(1024)S(1)} %get-tuple-element.197, bf16[1,512,16]{1,0,2:T(2,128)(2,1)S(1)} %constant_dynamic-slice_fusion.5), kind=kOutput, calls=%fused_computation.9.clone.1 | convolution fusion | flops 23625728 | bytes 4218880 | tf_op jit(solution)/shard_map/while/body/eval_jaxpr/dot_general | solution.py:96
  124.8 1.5 fusion.64
  126.3 0.6 multiply_reduce_fusion.3
  127.0 10.5 %fusion.63 = (bf16[1,1,512,1024]{3,2,1,0:T(8,128)(2,1)S(1)}, bf16[1,1,512,1024]{3,2,1,0:T(8,128)(2,1)S(1)}) fusion(f32[512,1024]{1,0:T(8,128)S(1)} %multiply_reduce_fusion.3, f32[1024]{0:T(1024)S(1)} %get-tuple-element.194, s32[1024]{0:T(1024)S(1)} %get-tuple-element.197, bf16[1,512,16]{1,0,2:T(2,128)(2,1)S(1)} %constant_dynamic-slice_fusion.5), kind=kOutput, calls=%fused_computation.9.clone.1 | convolution fusion | flops 23625728 | bytes 4218880 | tf_op jit(solution)/shard_map/while/body/eval_jaxpr/dot_general | solution.py:96
  137.5 1.5 fusion.64
  139.0 0.6 multiply_reduce_fusion.3
  139.7 10.5 %fusion.63 = (bf16[1,1,512,1024]{3,2,1,0:T(8,128)(2,1)S(1)}, bf16[1,1,512,1024]{3,2,1,0:T(8,128)(2,1)S(1)}) fusion(f32[512,1024]{1,0:T(8,128)S(1)} %multiply_reduce_fusion.3, f32[1024]{0:T(1024)S(1)} %get-tuple-element.194, s32[1024]{0:T(1024)S(1)} %get-tuple-element.197, bf16[1,512,16]{1,0,2:T(2,128)(2,1)S(1)} %constant_dynamic-slice_fusion.5), kind=kOutput, calls=%fused_computation.9.clone.1 | convolution fusion | flops 23625728 | bytes 4218880 | tf_op jit(solution)/shard_map/while/body/eval_jaxpr/dot_general | solution.py:96
  150.3 1.5 fusion.64
  151.8 0.6 multiply_reduce_fusion.3
  152.5 10.5 %fusion.63 = (bf16[1,1,512,1024]{3,2,1,0:T(8,128)(2,1)S(1)}, bf16[1,1,512,1024]{3,2,1,0:T(8,128)(2,1)S(1)}) fusion(f32[512,1024]{1,0:T(8,128)S(1)} %multiply_reduce_fusion.3, f32[1024]{0:T(1024)S(1)} %get-tuple-element.194, s32[1024]{0:T(1024)S(1)} %get-tuple-element.197, bf16[1,512,16]{1,0,2:T(2,128)(2,1)S(1)} %constant_dynamic-slice_fusion.5), kind=kOutput, calls=%fused_computation.9.clone.1 | convolution fusion | flops 23625728 | bytes 4218880 | tf_op jit(solution)/shard_map/while/body/eval_jaxpr/dot_general | solution.py:96
  163.0 1.5 fusion.64
  164.5 0.5 cosine_multiply_fusion
  165.7 3.6 %fusion.14 = f32[48,4,512]{2,0,1:T(8,128)S(1)} fusion(bf16[4,2,512,1024]{3,2,0,1:T(8,128)(2,1)} %get-tuple-element.42, bf16[48,2048]{1,0:T(8,128)(2,1)S(1)} %maximum_maximum_fusion), kind=kOutput, calls=%fused_computation.24 | convolution fusion | flops 201326592 | bytes 4685824 | tf_op jit(solution)/shard_map/dot_general | solution.py:145
  169.3 3.6 %fusion.28 = f32[48,4,512]{2,0,1:T(8,128)S(1)} fusion(f32[48,4,512]{2,0,1:T(8,128)S(1)} %fusion.14, bf16[4,2,512,1024]{3,2,0,1:T(8,128)(2,1)} %get-tuple-element.42, bf16[48,2048]{1,0:T(8,128)(2,1)S(1)} %maximum_maximum_fusion), kind=kOutput, calls=%fused_computation.38 | convolution fusion | flops 201424896 | bytes 5079040 | tf_op jit(solution)/shard_map/dot_general | solution.py:139
  172.9 0.3 copy.117
  173.1 0.4 reshape_reshape.16
  173.6 0.2 fusion.42
  173.8 0.2 reduce_sum.116
  174.7 17.0 %all_to_all.30 = f32[32,1,768]{2,1,0:T(1,128)S(1)} all-to-all(f32[32,1,768]{2,1,0:T(1,128)S(1)} %reshape.155), channel_id=1, replica_groups=mesh['row'=16,'col'=32] {'col'}, dimensions={0} | all-to-all | bytes 196608 | tf_op jit(solution)/shard_map/all_to_all | solution.py:52
  191.7 0.5 broadcast.105
  192.2 0.9 reduce
  193.4 9.5 %all_to_all.31 = bf16[16,2,384]{2,1,0:T(2,128)(2,1)S(1)} all-to-all(bf16[16,2,384]{2,1,0:T(2,128)(2,1)S(1)} %reshape.157), channel_id=1, replica_groups=mesh['row'=16,'col'=32] {'row'}, dimensions={0} | all-to-all | bytes 49152 | tf_op jit(solution)/shard_map/all_to_all | solution.py:31
  203.5 3.6 %fusion.12 = f32[48,4,512]{2,0,1:T(8,128)S(1)} fusion(bf16[4,2,512,1024]{3,2,0,1:T(8,128)(2,1)} %get-tuple-element.42, bf16[48,2048]{1,0:T(8,128)(2,1)S(1)} %maximum_maximum_fusion.1), kind=kOutput, calls=%fused_computation.22 | convolution fusion | flops 201326592 | bytes 4685824 | tf_op jit(solution)/shard_map/dot_general | solution.py:145
  207.1 3.6 %fusion.31 = f32[48,4,512]{2,0,1:T(8,128)S(1)} fusion(f32[48,4,512]{2,0,1:T(8,128)S(1)} %fusion.12, bf16[4,2,512,1024]{3,2,0,1:T(8,128)(2,1)} %get-tuple-element.42, bf16[48,2048]{1,0:T(8,128)(2,1)S(1)} %maximum_maximum_fusion.1), kind=kOutput, calls=%fused_computation.39 | convolution fusion | flops 201424896 | bytes 5079040 | tf_op jit(solution)/shard_map/dot_general | solution.py:139
  210.7 0.3 copy.122
  210.9 0.4 reshape_reshape.17
  211.5 0.2 fusion.43
  212.5 16.9 %all_to_all.32 = f32[32,1,768]{2,1,0:T(1,128)S(1)} all-to-all(f32[32,1,768]{2,1,0:T(1,128)S(1)} %reshape.159), channel_id=1, replica_groups=mesh['row'=16,'col'=32] {'col'}, dimensions={0} | all-to-all | bytes 196608 | tf_op jit(solution)/shard_map/all_to_all | solution.py:52
  229.4 0.9 reduce.1
  230.7 9.5 %all_to_all.33 = bf16[16,2,384]{2,1,0:T(2,128)(2,1)S(1)} all-to-all(bf16[16,2,384]{2,1,0:T(2,128)(2,1)S(1)} %reshape.161), channel_id=1, replica_groups=mesh['row'=16,'col'=32] {'row'}, dimensions={0} | all-to-all | bytes 49152 | tf_op jit(solution)/shard_map/all_to_all | solution.py:31
  240.8 3.6 %fusion.10 = f32[48,4,512]{2,0,1:T(8,128)S(1)} fusion(bf16[4,2,512,1024]{3,2,0,1:T(8,128)(2,1)} %get-tuple-element.42, bf16[48,2048]{1,0:T(8,128)(2,1)S(1)} %maximum_maximum_fusion.2), kind=kOutput, calls=%fused_computation.20 | convolution fusion | flops 201326592 | bytes 4685824 | tf_op jit(solution)/shard_map/dot_general | solution.py:145
  244.4 3.6 %fusion.34 = f32[48,4,512]{2,0,1:T(8,128)S(1)} fusion(f32[48,4,512]{2,0,1:T(8,128)S(1)} %fusion.10, bf16[4,2,512,1024]{3,2,0,1:T(8,128)(2,1)} %get-tuple-element.42, bf16[48,2048]{1,0:T(8,128)(2,1)S(1)} %maximum_maximum_fusion.2), kind=kOutput, calls=%fused_computation.40 | convolution fusion | flops 201424896 | bytes 5079040 | tf_op jit(solution)/shard_map/dot_general | solution.py:139
  247.9 0.3 copy.129
  248.2 0.4 reshape_reshape.18
  248.7 0.2 fusion.44
  249.8 16.9 %all_to_all.34 = f32[32,1,768]{2,1,0:T(1,128)S(1)} all-to-all(f32[32,1,768]{2,1,0:T(1,128)S(1)} %reshape.163), channel_id=1, replica_groups=mesh['row'=16,'col'=32] {'col'}, dimensions={0} | all-to-all | bytes 196608 | tf_op jit(solution)/shard_map/all_to_all | solution.py:52
  266.7 0.9 reduce.2
  267.8 0.6 add.37
  (108 shorter events, 6.1 us)
Async XLA Ops:
  1.4 163.6 %all-to-all-start = ((bf16[16,2,384]{2,1,0:T(2,128)(2,1)}), bf16[16,2,384]{2,1,0:T(2,128)(2,1)S(1)}, u32[]{:S(2)}, u32[]{:S(2)}) async-start(bf16[16,2,384]{2,1,0:T(2,128)(2,1)} %reshape.153), calls=%async_computation | async-start | bytes 49152 | tf_op jit(solution)/shard_map/all_to_all | solution.py:31
  172.8 20.4 %copy-start = (f32[2,3,2,64]{3,2,1,0:T(2,128)S(1)}, f32[2,3,2,64]{3,2,1,0:T(2,128)}, u32[]{:S(2)}) copy-start(f32[2,3,2,64]{3,2,1,0:T(2,128)} %param.10) | copy-start | bytes 9220
where the time goes:
time: 269 us; the launch traced here: 268 us
  blocking collectives  169 us (63%)
  matrix products  63.4 us (24%)
  other arithmetic  16.9 us (6%)
  starting transfers between devices  10.4 us (4%)
  local copies, waits for them, and re-layouts  8.11 us (3%)
    all_gather x2, blocking collectives, rows_first(): whole = lax.all_gather(both, axis, axis=0, tiled=True)  99 us
    all_to_all x3, blocking collectives, summed_on_arrival(): tiles = lax.all_to_all(cut_along(shard, dim, count), axis, 0, 0, tiled=True)  50.8 us
    dot_general x4, matrix products, kernel_block(): jnp.dot(visible_rows, tiles_onehot, preferred_element_type=jnp.float32)  42 us
    all_to_all x2, blocking collectives, sent_to_all(): return lax.all_to_all(copies, axis, split_axis=0, concat_axis=0, tiled=True)  19 us
    dot_general x3, matrix products, shards(): lax.dot_general(operand[:, :part_len], kernel_all[:, 0], (((1,), (2,)), (...  10.7 us
    dot_general x3, matrix products, shards(): lax.dot_general(operand[:, part_len:], kernel_all[:, 1], (((1,), (2,)), (...  10.7 us
    all_to_all x1, starting transfers between devices, sent_to_all(): return lax.all_to_all(copies, axis, split_axis=0, concat_axis=0, tiled=True)  10.4 us
    dynamic_update_slice x4, other arithmetic, shards(): kernel_all = lax.map(one_block, (obs_blocks, row_blocks))  5.94 us
  transfers between devices with their start and end apart: 1, of which 0 were waited for; matrix products, arithmetic and copies ran while one was open for 20% of the time, Pallas kernels for 0%

commit v1 on v0

v1 whole, which is shorter than its diff:
```python
import functools
import math

import jax
import jax.numpy as jnp
from jax import lax
from jax.experimental import pallas as pl
from jax.experimental.pallas import tpu as pltpu
from jax.sharding import PartitionSpec as P

ITERS = 3
TILE = 64
MESH = pl.DeviceIdType.MESH
F32, BF16 = jnp.float32, jnp.bfloat16

NX, NY, NZ, NC = 4, 8, 8, 2
Z_ORDER = (0, 1, 7, 2, 6, 3, 5, 4)
NEAR_Z = 5
NOBS = NY * NC * TILE
NSRC = NX * NZ * TILE
NEAR = NEAR_Z * NX * TILE
FAR = NSRC - NEAR
DEPTH = 64
BLOCK = 256
BIG = 2.0**127

YC = tuple((y, c) for y in (4, 3, 5, 2, 6, 1, 7, 0) for c in (1, 0) if y or c)
XZ = tuple(
    (x, z)
    for x, z in sorted(
        ((x, z) for x in range(NX) for z in range(NZ) if x or z),
        key=lambda p: -(min(p[0], NX - p[0]) + min(p[1], NZ - p[1])),
    )
)


def src_slot(x, z):
    return Z_ORDER.index(z % NZ) * NX + x % NX


def split3(v):
    high = v.astype(BF16).astype(F32)
    rest = v - high
    mid = rest.astype(BF16).astype(F32)
    return high, mid, (rest - mid).astype(BF16).astype(F32)


def pair_kernel(sq):
    inv = lax.rsqrt(sq)
    turns = sq * inv
    part = turns - jnp.round(turns)
    u = part * part
    half_sin = part * (3.14158208 + u * (-5.1671442 + u * (2.5419089 + u * -0.55465701)))
    half_cos = 0.9999933 + u * (-4.93393802 + u * (4.04128384 + u * -1.22212701))
    sine = half_sin * half_cos
    cosine = 0.5 - half_sin * half_sin
    z = inv * (1.0 / (2.0 * math.pi))
    a = inv * inv
    return (a * (sine + z * cosine)).astype(BF16), (a * (cosine - z * sine)).astype(BF16)


def body(
    pos_ref, ori_ref, area_ref, inc_ref, vis_ref, out_ref,
    st_obs, rx_obs, st_pw, rx_pw, st_vis, rx_vis, st_cur, rx_cur, st_sum, rx_sum,
    inc_pack, obs_all, pw_all, right_t, right, left, s_a, s_b, k_all, x_near, x_far, acc,
    send_sem, recv_sem,
):
    row, col = lax.axis_index("row"), lax.axis_index("col")
    x0, zl0 = lax.rem(row, NX), row // NX
    y0, zh0, c0 = col // 4, lax.rem(col // 2, 2), lax.rem(col, 2)
    z0 = zh0 * 4 + zl0

    def device(dx=0, dy=0, dz=0, dc=0):
        x, y, z, c = lax.rem(x0 + dx, NX), lax.rem(y0 + dy, NY), lax.rem(z0 + dz, NZ), lax.rem(c0 + dc, NC)
        return {"row": lax.rem(z, 4) * NX + x, "col": y * 4 + (z // 4) * 2 + c}

    barrier = pltpu.get_barrier_semaphore()
    for x, z in XZ:
        pl.semaphore_signal(barrier, inc=1, device_id=device(dx=x, dz=z), device_id_type=MESH)
    for y, c in YC:
        pl.semaphore_signal(barrier, inc=1, device_id=device(dy=y, dc=c), device_id_type=MESH)

    lane = lax.broadcasted_iota(jnp.int32, (8, 128), 1)
    sub = lax.broadcasted_iota(jnp.int32, (8, 128), 0)
    low = lane < TILE
    top = sub < 4

    def swap_halves(v):
        return pltpu.roll(v, TILE, axis=1)

    def wide(v):
        return jnp.concatenate([v, jnp.zeros((v.shape[0], 128 - v.shape[1]), v.dtype)], axis=1)

    pos = pos_ref[...]
    polar, azimuth = ori_ref[0:1, :], ori_ref[1:2, :]
    sin_p = jnp.sin(polar)
    st_obs[0] = jnp.zeros((8, 128), F32)
    st_obs[0, 0:3, 0:TILE] = pos
    st_obs[0, 3:4, 0:TILE] = sin_p * jnp.cos(azimuth)
    st_obs[0, 4:5, 0:TILE] = sin_p * jnp.sin(azimuth)
    st_obs[0, 5:6, 0:TILE] = jnp.cos(polar)
    st_obs[1] = swap_halves(st_obs[0])
    rx_obs[0] = st_obs[0]
    acc[0:8, 0:128] = jnp.zeros((8, 128), F32)
    acc[0:3, 0:TILE] = pos
    acc[3:4, 0:TILE] = area_ref[...] * (2.0 * 64.0 / math.sqrt(32768.0))
    own_pw = acc[0:8, 0:128]
    st_pw[0] = own_pw[0:4]
    st_pw[1] = swap_halves(own_pw)[0:4]
    rx_pw[0] = own_pw[0:4]
    st_vis[...] = jnp.concatenate([wide(vis_ref[b].astype(F32)) for b in range(16)], axis=0).astype(BF16)

    inc_pack[...] = jnp.zeros((8, 128), F32)
    for k in range(2):
        inc_pack[4 * k : 4 * k + 2, 0:TILE] = inc_ref[0, k]
        inc_pack[4 * k + 2 : 4 * k + 4, 0:TILE] = inc_ref[1, k]
    third = jnp.concatenate([inc_ref[0, 2], inc_ref[1, 2], jnp.zeros((4, TILE), F32)], axis=0)
    inc_pack[...] += swap_halves(wide(third))

    def stage_current(bounce, packed):
        st_cur[bounce, 0] = packed.astype(BF16)
        st_cur[bounce, 1] = swap_halves(packed).astype(BF16)
        rx_cur[bounce, 0] = st_cur[bounce, 0]

    stage_current(0, inc_pack[...])

    pl.semaphore_wait(barrier, len(XZ) + len(YC))

    def send(src, dst, sem, **offset):
        pltpu.make_async_remote_copy(
            src_ref=src, dst_ref=dst, send_sem=send_sem.at[sem], recv_sem=recv_sem.at[sem],
            device_id=device(**offset), device_id_type=MESH,
        ).start()

    def arrived(ref, sem):
        pltpu.make_async_copy(ref, ref, recv_sem.at[sem]).wait()

    def left_here(ref, sem):
        pltpu.make_async_copy(ref, ref, send_sem.at[sem]).wait()

    near_slots, far_slots = NEAR_Z * NX, (NZ - NEAR_Z) * NX
    S_OBS, S_VIS, S_PWN, S_PWF, S_CUR, S_SUM = 0, 1, 2, 3, 4, 10

    def sem_of(base, x, z):
        return base if src_slot(-x, -z) < near_slots else base + 1

    for x, z in XZ:
        send(st_pw.at[x % 2], rx_pw.at[src_slot(-x, -z)], sem_of(S_PWN, x, z), dx=x, dz=z)
    send(st_vis, rx_vis, S_VIS, dz=4)
    for y, c in YC:
        send(st_obs.at[c], rx_obs.at[(-y % NY) * NC + c], S_OBS, dy=y, dc=c)

    def send_current(bounce):
        for x, z in XZ:
            send(
                st_cur.at[bounce, x % 2], rx_cur.at[bounce, src_slot(-x, -z)],
                sem_of(S_CUR + 2 * bounce, x, z), dx=x, dz=z,
            )

    send_current(0)

    slot = lax.broadcasted_iota(jnp.int32, (32, 16), 0)
    there = lax.broadcasted_iota(jnp.int32, (32, 16), 1)
    place = slot // NX
    z_off = jnp.where(lax.rem(place, 2) == 1, (place + 1) // 2, lax.rem(NZ - place // 2, NZ))
    z_of = lax.rem(z0 + z_off, NZ)
    match = there == lax.rem(z_of, 4) * NX + lax.rem(x0 + lax.rem(slot, NX), NX)
    own_z = (z_of // 4) == zh0
    pick_own = jnp.where(match & own_z, 1.0, 0.0).astype(BF16)
    pick_far = jnp.where(match & jnp.logical_not(own_z), 1.0, 0.0).astype(BF16)
    a_row = lax.broadcasted_iota(jnp.int32, (128, NOBS), 0)
    a_lane = lax.broadcasted_iota(jnp.int32, (128, NOBS), 1)
    a_of = (
        lax.rem(y0 + a_lane // 128, NY) * 4 + zh0 * 2 + lax.rem(c0 + lax.rem(a_lane // TILE, 2), 2)
    )
    spread = jnp.where(a_row == a_of, 1.0, 0.0).astype(BF16)

    right_t[...] = jnp.zeros((128, NSRC), F32)
    right_t[18:24, :] = jnp.ones((6, NSRC), F32)
    b_row = lax.broadcasted_iota(jnp.int32, (32, NSRC), 0)
    b_lane = lax.broadcasted_iota(jnp.int32, (32, NSRC), 1)
    right_t[24:56, :] = jnp.where(b_row == b_lane // TILE, 1.0, 0.0)

    arrived(rx_obs.at[pl.ds(1, NY * NC - 1)], S_OBS)
    for y in range(NY):
        obs_all[:, y * 128 : (y + 1) * 128] = rx_obs[2 * y] + rx_obs[2 * y + 1]
    big_pos = 4.0 * obs_all[0:3, :]
    h, m, l = split3(big_pos)
    for i, part in enumerate((h, m, l, h, m, h)):
        left[3 * i : 3 * i + 3, :] = part
    left[18:21, :] = jnp.ones((3, NOBS), F32)
    norms = split3(jnp.sum(big_pos * big_pos, axis=0, keepdims=True) + 16.0 * 0.0025)
    for i, part in enumerate(norms):
        left[21 + i : 22 + i, :] = part
    arrived(rx_vis, S_VIS)
    seen = jnp.dot(pick_own, st_vis[...], preferred_element_type=F32) + jnp.dot(
        pick_far, rx_vis[...], preferred_element_type=F32
    )
    seen_all = jnp.dot(seen.astype(BF16), spread, preferred_element_type=F32)
    left[24:56, :] = BIG * (1.0 - seen_all)
    left[56:64, :] = jnp.zeros((8, NOBS), F32)

    arrived(rx_pw.at[pl.ds(1, near_slots - 1)], S_PWN)
    arrived(rx_pw.at[pl.ds(near_slots, far_slots)], S_PWF)
    for g in range(NSRC // 128):
        pw_all[:, g * 128 : (g + 1) * 128] = rx_pw[2 * g] + rx_pw[2 * g + 1]
    big_src = 4.0 * pw_all[0:3, :]
    h, m, l = split3(big_src)
    for i, part in enumerate((h, h, h, m, m, l)):
        right_t[3 * i : 3 * i + 3, :] = -2.0 * part
    norms = split3(jnp.sum(big_src * big_src, axis=0, keepdims=True))
    for i, part in enumerate(norms):
        right_t[18 + i : 19 + i, :] = part
    for g in range(NSRC // 128):
        right[g * 128 : (g + 1) * 128, :] = jnp.transpose(right_t[:, g * 128 : (g + 1) * 128]).astype(BF16)

    def operand(bounce, groups, first, x_ref):
        span = len(groups) * 128
        for g in groups:
            lanes = slice(g * 128, (g + 1) * 128)
            even, odd = rx_cur[bounce, 2 * g].astype(F32), rx_cur[bounce, 2 * g + 1].astype(F32)
            same = jnp.where(low, even, odd)
            s = (same, pltpu.roll(same, 4, axis=0), swap_halves(jnp.where(low, odd, even)))
            p = [pw_all[k : k + 1, lanes] for k in range(3)]
            w = pw_all[3:4, lanes]
            rows = []
            turned = []
            for k in range(3):
                i, j = (k + 1) % 3, (k + 2) % 3
                cross = p[i] * s[j] - p[j] * s[i]
                both = jnp.where(top, s[k], pltpu.roll(cross, 4, axis=0)) * w
                rows.append(both)
                turned.append(
                    jnp.where(lax.rem(sub, 4) < 2, -pltpu.roll(both, 6, axis=0), pltpu.roll(both, 2, axis=0))
                )
            at = (g - first) * 128
            x_ref[:, at : at + 128] = jnp.concatenate(rows, axis=0).astype(BF16)
            x_ref[:, span + at : span + at + 128] = jnp.concatenate(turned, axis=0).astype(BF16)

    near_groups = range(0, NEAR // 128)
    far_groups = range(NEAR // 128, NSRC // 128)

    def near_operand(bounce):
        arrived(rx_cur.at[bounce, pl.ds(1, near_slots - 1)], S_CUR + 2 * bounce)
        operand(bounce, near_groups, 0, x_near)

    def far_operand(bounce):
        arrived(rx_cur.at[bounce, pl.ds(near_slots, far_slots)], S_CUR + 2 * bounce + 1)
        operand(bounce, far_groups, NEAR // 128, x_far)

    def near_product(lanes):
        return jnp.dot(x_near[...], k_all[0 : 2 * NEAR, lanes], preferred_element_type=F32)

    def far_product(lanes):
        return jnp.dot(x_far[...], k_all[2 * NEAR : 2 * NSRC, lanes], preferred_element_type=F32)

    def messages(bounce, y, total):
        lanes = slice(y * 128, (y + 1) * 128)
        p = [obs_all[k : k + 1, lanes] for k in range(3)]
        n = [obs_all[3 + k : 4 + k, lanes] for k in range(3)]
        a = [total[8 * k : 8 * k + 8, :] for k in range(3)]
        d = [
            p[(k + 1) % 3] * a[(k + 2) % 3] - p[(k + 2) % 3] * a[(k + 1) % 3] - pltpu.roll(a[k], 4, axis=0)
            for k in range(3)
        ]
        s = [n[(k + 1) % 3] * d[(k + 2) % 3] - n[(k + 2) % 3] * d[(k + 1) % 3] for k in range(3)]
        pair = jnp.where(top, s[0], pltpu.roll(s[1], 4, axis=0))
        for c, packed in (
            (0, jnp.where(low, pair, swap_halves(s[2]))),
            (1, jnp.where(low, swap_halves(pair), s[2])),
        ):
            if y == 0 and c == 0:
                rx_sum[bounce, 0] = packed.astype(BF16)
            else:
                st_sum[bounce, 2 * y + c] = packed.astype(BF16)
                send(
                    st_sum.at[bounce, 2 * y + c], rx_sum.at[bounce, (-y % NY) * NC + c],
                    S_SUM + bounce, dy=y, dc=c,
                )

    blocks = NSRC // BLOCK
    steps = (NOBS // BLOCK) * blocks

    def squares(step, ref):
        step = lax.rem(step, steps)
        rows = pl.ds(pl.multiple_of(lax.rem(step, blocks) * BLOCK, BLOCK), BLOCK)
        lanes = pl.ds(pl.multiple_of((step // blocks) * BLOCK, BLOCK), BLOCK)
        ref[...] = jnp.dot(
            right[rows, 0:DEPTH], left[:, lanes].astype(BF16), preferred_element_type=F32
        )

    def fill(ref, block, q):
        re_row = pl.multiple_of(block * BLOCK + jnp.where(block < NEAR // BLOCK, 0, NEAR), BLOCK)
        im_row = pl.multiple_of(block * BLOCK + jnp.where(block < NEAR // BLOCK, NEAR, NSRC), BLOCK)
        for r in range(0, BLOCK, 64):
            for v in range(0, BLOCK, 128):
                re, im = pair_kernel(ref[r : r + 64, v : v + 128])
                k_all[pl.ds(re_row + r, 64), q * BLOCK + v : q * BLOCK + v + 128] = re
                k_all[pl.ds(im_row + r, 64), q * BLOCK + v : q * BLOCK + v + 128] = im

    quarters = (2, 1, 3, 0)
    near_operand(0)
    far_operand(0)
    squares(jnp.int32(quarters[0] * blocks), s_a)
    for n, q in enumerate(quarters):
        after = quarters[(n + 1) % len(quarters)]

        def two(i, _, q=q, after=after):
            squares(q * blocks + 2 * i + 1, s_b)
            fill(s_a, 2 * i, q)
            squares(jnp.where(2 * i + 2 < blocks, q * blocks + 2 * i + 2, after * blocks), s_a)
            fill(s_b, 2 * i + 1, q)
            return 0

        lax.fori_loop(0, blocks // 2, two, 0)
        lanes = slice(q * BLOCK, (q + 1) * BLOCK)
        total = near_product(lanes) + far_product(lanes)
        for y in (2 * q + 1, 2 * q):
            messages(0, y, total[:, (y % 2) * 128 : (y % 2) * 128 + 128])

    current = None
    for bounce in range(ITERS):
        if bounce > 0:
            near_operand(bounce)
            for q in quarters:
                lanes = slice(q * BLOCK, (q + 1) * BLOCK)
                acc[:, lanes] = near_product(lanes)
            far_operand(bounce)
            for q in quarters:
                lanes = slice(q * BLOCK, (q + 1) * BLOCK)
                total = acc[:, lanes] + far_product(lanes)
                for y in (2 * q + 1, 2 * q):
                    messages(bounce, y, total[:, (y % 2) * 128 : (y % 2) * 128 + 128])
        arrived(rx_sum.at[bounce, pl.ds(1, NY * NC - 1)], S_SUM + bounce)
        current = inc_pack[...] + jnp.sum(rx_sum[bounce].astype(F32), axis=0)
        if bounce + 1 < ITERS:
            stage_current(bounce + 1, current)
            send_current(bounce + 1)

    third = swap_halves(current)
    for part in range(2):
        for k in range(2):
            out_ref[part, k] = current[4 * k + 2 * part : 4 * k + 2 * part + 2, 0:TILE]
        out_ref[part, 2] = third[2 * part : 2 * part + 2, 0:TILE]

    left_here(rx_obs.at[pl.ds(1, NY * NC - 1)], S_OBS)
    left_here(rx_vis, S_VIS)
    left_here(rx_pw.at[pl.ds(1, near_slots - 1)], S_PWN)
    left_here(rx_pw.at[pl.ds(near_slots, far_slots)], S_PWF)
    for bounce in range(ITERS):
        left_here(rx_cur.at[bounce, pl.ds(1, near_slots - 1)], S_CUR + 2 * bounce)
        left_here(rx_cur.at[bounce, pl.ds(near_slots, far_slots)], S_CUR + 2 * bounce + 1)
        left_here(rx_sum.at[bounce, pl.ds(1, NY * NC - 1)], S_SUM + bounce)


def shards(positions, orient, areas, incident, visible):
    vmem = pltpu.VMEM
    scratch = [
        vmem((2, 8, 128), F32), vmem((16, 8, 128), F32),
        vmem((2, 4, 128), F32), vmem((32, 4, 128), F32),
        vmem((16, 128), BF16), vmem((16, 128), BF16),
        vmem((ITERS, 2, 8, 128), BF16), vmem((ITERS, 32, 8, 128), BF16),
        vmem((ITERS, 16, 8, 128), BF16), vmem((ITERS, 16, 8, 128), BF16),
        vmem((8, 128), F32), vmem((8, NOBS), F32), vmem((4, NSRC), F32),
        vmem((128, NSRC), F32), vmem((NSRC, 128), BF16), vmem((DEPTH, NOBS), F32),
        vmem((BLOCK, BLOCK), F32), vmem((BLOCK, BLOCK), F32),
        vmem((2 * NSRC, NOBS), BF16),
        vmem((24, 2 * NEAR), BF16), vmem((24, 2 * FAR), BF16), vmem((24, NOBS), F32),
        pltpu.SemaphoreType.DMA((13,)), pltpu.SemaphoreType.DMA((13,)),
    ]
    return pl.pallas_call(
        body,
        out_shape=jax.ShapeDtypeStruct(incident.shape, F32),
        in_specs=[pl.BlockSpec(memory_space=vmem)] * 5,
        out_specs=pl.BlockSpec(memory_space=vmem),
        scratch_shapes=scratch,
        compiler_params=pltpu.CompilerParams(
            collective_id=0, has_side_effects=True, vmem_limit_bytes=48 * 2**20
        ),
        cost_estimate=pl.CostEstimate(flops=3_000_000_000, bytes_accessed=1_000_000, transcendentals=4_000_000),
    )(positions, orient, areas.reshape(1, -1), incident, jnp.transpose(visible, (1, 2, 0)))


def solution(mesh):
    in_specs = (
        P(None, ("row", "col")),
        P(None, ("row", "col")),
        P(("row", "col")),
        P(None, None, None, ("row", "col")),
        P("row", None, "col"),
    )
    out_specs = P(None, None, None, ("row", "col"))
    return jax.shard_map(shards, mesh=mesh, in_specs=in_specs, out_specs=out_specs, check_vma=False)
```

time: 269 us -> 66.6 us (0.25)
  blocking collectives: 169 us -> 0 us
  Pallas kernels: 0 us -> 63.7 us
  matrix products: 63.4 us -> 0 us
  other arithmetic: 16.9 us -> 0 us
  starting transfers between devices: 10.4 us -> 0 us
  local copies, waits for them, and re-layouts: 8.11 us -> 2.68 us
    all_gather x2 -> x0, blocking collectives: 99 us -> none  [rows_first(): whole = lax.all_gather(both, axis, axis=0, tiled=True)]
    all_to_all x5 -> x0, blocking collectives: 69.8 us -> none  [the longest x3 50.8 us: summed_on_arrival(): tiles = lax.all_to_all(cut_along(shard, dim, count), axis, 0, 0, tiled=True)]
    pallas_call x0 -> x1, Pallas kernels: none -> 63.7 us  [shards(): pl.pallas_call(body, out_shape=jax.ShapeDtypeStruct(incident.shape, F32),...]
    dot_general x10 -> x0, matrix products: 63.4 us -> none  [the longest x4 42 us: kernel_block(): jnp.dot(visible_rows, tiles_onehot, preferred_element_type=jnp.float32)]
    all_to_all x1 -> x0, starting transfers between devices: 10.4 us -> none  [sent_to_all(): return lax.all_to_all(copies, axis, split_axis=0, concat_axis=0, tiled=True)]
    dynamic_update_slice x4 -> x0, other arithmetic: 5.94 us -> none  [shards(): kernel_all = lax.map(one_block, (obs_blocks, row_blocks))]
    reduce_sum x14 -> x0, other arithmetic: 3.47 us -> none  [the longest x4 2.56 us: kernel_block(): dist_square = jnp.sum(separation * separation, axis=0) + soft_square]
  transfers between devices with their start and end apart: 1 -> 0, of which waited for: 0 -> 0; matrix products, arithmetic and copies ran while one was open for 20% -> 0% of each run, Pallas kernels for 0% -> 0%
where the time goes in v1:
time: 66.6 us; the launch traced here: 66.4 us
  Pallas kernels  63.7 us (96%)
  local copies, waits for them, and re-layouts  2.68 us (4%)
    pallas_call x1, Pallas kernels, shards(): pl.pallas_call(body, out_shape=jax.ShapeDtypeStruct(incident.shape, F32),...  63.7 us
    unnamed x11, local copies, waits for them, and re-layouts  2.68 us

profile of v1, /device:TPU:1, one launch (start us, length us, event | category | flops | bytes accessed | tf_op | source)
XLA Modules:
  0.0 66.4 jit_solution(7527532631206098223)
XLA Ops:
  0.0 0.0 copy-start.2
  0.0 0.0 copy-start.3
  0.0 0.0 copy-start.4
  0.0 0.7 %copy-done.2 = f32[3,64]{1,0:T(4,128)S(1)} copy-done((f32[3,64]{1,0:T(4,128)S(1)}, f32[3,64]{1,0:T(4,128)}, u32[]{:S(2)}) %copy-start.2) | copy-done | bytes 792
  0.7 0.0 copy-done.3
  0.7 0.0 copy-done.4
  0.7 0.0 copy-start
  0.7 0.7 %copy-done = s32[32,16,1]{0,2,1:T(1,128)S(1)} copy-done((s32[32,16,1]{0,2,1:T(1,128)S(1)}, s32[32,16,1]{0,2,1:T(1,128)}, u32[]{:S(2)}) %copy-start) | copy-done | bytes 2072
  1.4 0.0 copy-start.1
  1.4 0.7 %copy-done.1 = f32[2,3,2,64]{3,2,1,0:T(2,128)S(1)} copy-done((f32[2,3,2,64]{3,2,1,0:T(2,128)S(1)}, f32[2,3,2,64]{3,2,1,0:T(2,128)}, u32[]{:S(2)}) %copy-start.1) | copy-done | bytes 3096
  2.1 63.7 %shard_map.55 = f32[2,3,2,64]{3,2,1,0:T(2,128)S(1)} custom-call(f32[3,64]{1,0:T(4,128)S(1)} %copy-done.2, f32[2,64]{1,0:T(2,128)S(1)} %copy-done.3, f32[1,64]{1,0:T(1,128)S(1)} %bitcast.3, f32[2,3,2,64]{3,2,1,0:T(2,128)S(1)} %copy-done.1, s32[16,1,32]{2,1,0:T(1,128)S(1)} %bitcast.2), custom_call_target="tpu_custom_call" | custom-call | flops 3000000000 | bytes 1000000 | tf_op jit(solution)/shard_map/pallas_call | solution.py:371
  65.8 0.6 copy.7
Async XLA Ops:
  0.0 0.7 %copy-start.2 = (f32[3,64]{1,0:T(4,128)S(1)}, f32[3,64]{1,0:T(4,128)}, u32[]{:S(2)}) copy-start(f32[3,64]{1,0:T(4,128)} %pos_ref.1) | copy-start | bytes 2308
  0.0 0.7 %copy-start.3 = (f32[2,64]{1,0:T(2,128)S(1)}, f32[2,64]{1,0:T(2,128)}, u32[]{:S(2)}) copy-start(f32[2,64]{1,0:T(2,128)} %ori_ref.1) | copy-start | bytes 1540
  0.0 0.7 %copy-start.4 = (f32[64]{0:T(128)S(1)}, f32[64]{0:T(128)}, u32[]{:S(2)}) copy-start(f32[64]{0:T(128)} %param.7) | copy-start | bytes 772
  0.7 0.7 %copy-start = (s32[32,16,1]{0,2,1:T(1,128)S(1)}, s32[32,16,1]{0,2,1:T(1,128)}, u32[]{:S(2)}) copy-start(s32[32,16,1]{0,2,1:T(1,128)} %param.9) | copy-start | bytes 6148
  1.4 0.7 %copy-start.1 = (f32[2,3,2,64]{3,2,1,0:T(2,128)S(1)}, f32[2,3,2,64]{3,2,1,0:T(2,128)}, u32[]{:S(2)}) copy-start(f32[2,3,2,64]{3,2,1,0:T(2,128)} %inc_ref.1) | copy-start | bytes 9220

commit v2 on v1

v2 whole, which is shorter than its diff:
```python
import math

import jax
import jax.numpy as jnp
from jax import lax
from jax.experimental import pallas as pl
from jax.experimental.pallas import tpu as pltpu
from jax.sharding import PartitionSpec as P

ITERS = 3
TILE = 64
MESH = pl.DeviceIdType.MESH
F32, BF16 = jnp.float32, jnp.bfloat16

NX, NY, NZ, NC = 4, 8, 8, 2
RING_ORDER = (0, 1, 7, 2, 6, 3, 5, 4)
NEAR_Z = 5
NOBS = NY * NC * TILE
NSRC = NX * NZ * TILE
NEAR = NEAR_Z * NX * TILE
FAR = NSRC - NEAR
DEPTH = 64
BLOCK = 256
HALF = NOBS // 2
ROWS = 48
BIG = 2.0**127

YC = tuple((y, c) for y in (4, 3, 5, 2, 6, 1, 7, 0) for c in (1, 0) if y or c)
XZ = tuple(
    (x, z)
    for x, z in sorted(
        ((x, z) for x in range(NX) for z in range(NZ) if x or z),
        key=lambda p: -(min(p[0], NX - p[0]) + min(p[1], NZ - p[1])),
    )
)


def src_slot(x, z):
    return RING_ORDER.index(z % NZ) * NX + x % NX


def obs_slot(y, c):
    return RING_ORDER.index(y % NY) * NC + c % NC


def ring_offset(place):
    return jnp.where(lax.rem(place, 2) == 1, (place + 1) // 2, lax.rem(8 - place // 2, 8))


def aligned(v, n):
    return v if isinstance(v, int) else pl.multiple_of(v, n)


def either(which, a, b):
    return (a if which else b) if isinstance(which, bool) else jnp.where(which, a, b)


def split3(v):
    high = v.astype(BF16).astype(F32)
    rest = v - high
    mid = rest.astype(BF16).astype(F32)
    return high, mid, (rest - mid).astype(BF16).astype(F32)


def pair_kernel(sq):
    inv = lax.rsqrt(sq)
    halves = sq * inv
    whole = jnp.round(halves)
    part = (halves - whole).astype(BF16)
    count = whole.astype(BF16)
    odd = count - ((count + BF16(384.0)) - BF16(384.0))
    a = (inv * inv).astype(BF16) * (BF16(1.0) - BF16(2.0) * (odd * odd))
    z = inv.astype(BF16) * BF16(1.0 / math.pi)
    u = part * part
    sine = part * (BF16(3.14064334) + u * (BF16(-5.13694906) + u * BF16(2.29967451)))
    cosine = BF16(0.99940325) + u * (BF16(-4.89118702) + u * BF16(3.58384395))
    return a * (sine + z * cosine), a * (cosine - z * sine)


def body(
    pos_hbm, ori_hbm, area_hbm, inc_hbm, vis_hbm, out_ref,
    pos_ref, ori_ref, area_ref, inc_ref, vis_ref, st_obs, rx_obs, st_pw, rx_pw, st_vis, rx_vis, st_cur, rx_cur, st_sum, rx_sum,
    inc_pack, obs_all, pw_all, right_t, right, left_f, left, s_a, s_b, k_all, x_near, x_far, acc,
    load_sem, send_sem, recv_sem,
):
    row, col = lax.axis_index("row"), lax.axis_index("col")
    x0, zl0 = lax.rem(row, NX), row // NX
    y0, zh0, c0 = col // 4, lax.rem(col // 2, 2), lax.rem(col, 2)
    z0 = zh0 * 4 + zl0

    def device(dx=0, dy=0, dz=0, dc=0):
        x, y, z, c = lax.rem(x0 + dx, NX), lax.rem(y0 + dy, NY), lax.rem(z0 + dz, NZ), lax.rem(c0 + dc, NC)
        return {"row": lax.rem(z, 4) * NX + x, "col": y * 4 + (z // 4) * 2 + c}

    loads = [
        pltpu.make_async_copy(src, dst, load_sem.at[i])
        for i, (src, dst) in enumerate(
            ((pos_hbm, pos_ref), (ori_hbm, ori_ref), (area_hbm, area_ref), (vis_hbm, vis_ref), (inc_hbm, inc_ref))
        )
    ]
    for load in loads:
        load.start()
    barrier = pltpu.get_barrier_semaphore()
    for x, z in XZ:
        pl.semaphore_signal(barrier, inc=1, device_id=device(dx=x, dz=z), device_id_type=MESH)
    for y, c in YC:
        pl.semaphore_signal(barrier, inc=1, device_id=device(dy=y, dc=c), device_id_type=MESH)

    lane = lax.broadcasted_iota(jnp.int32, (8, 128), 1)
    sub = lax.broadcasted_iota(jnp.int32, (8, 128), 0)
    low = lane < TILE
    top = sub < 4

    def swap_halves(v):
        return pltpu.roll(v, TILE, axis=1)

    def wide(v):
        return jnp.concatenate([v, jnp.zeros((v.shape[0], 128 - v.shape[1]), v.dtype)], axis=1)

    for load in loads:
        load.wait()

    pos = pos_ref[...]
    polar, azimuth = ori_ref[0:1, :], ori_ref[1:2, :]
    sin_p = jnp.sin(polar)
    st_obs[0] = jnp.zeros((8, 128), F32)
    st_obs[0, 0:3, 0:TILE] = pos
    st_obs[0, 3:4, 0:TILE] = sin_p * jnp.cos(azimuth)
    st_obs[0, 4:5, 0:TILE] = sin_p * jnp.sin(azimuth)
    st_obs[0, 5:6, 0:TILE] = jnp.cos(polar)
    st_obs[1] = swap_halves(st_obs[0])
    rx_obs[0] = st_obs[0]
    acc[0:8, 0:128] = jnp.zeros((8, 128), F32)
    acc[0:3, 0:TILE] = pos
    acc[3:4, 0:TILE] = area_ref[...] * (2.0 * 128.0 / math.sqrt(32768.0))
    own_pw = acc[0:8, 0:128]
    st_pw[0] = own_pw[0:4]
    st_pw[1] = swap_halves(own_pw)[0:4]
    rx_pw[0] = own_pw[0:4]
    st_vis[...] = jnp.concatenate([wide(vis_ref[b].astype(F32)) for b in range(16)], axis=0).astype(BF16)

    inc_pack[...] = jnp.zeros((8, 128), F32)
    for k in range(2):
        inc_pack[4 * k : 4 * k + 2, 0:TILE] = inc_ref[0, k]
        inc_pack[4 * k + 2 : 4 * k + 4, 0:TILE] = inc_ref[1, k]
    third = jnp.concatenate([inc_ref[0, 2], inc_ref[1, 2], jnp.zeros((4, TILE), F32)], axis=0)
    inc_pack[...] += swap_halves(wide(third))

    def stage_current(bounce, packed):
        st_cur[bounce, 0] = packed.astype(BF16)
        st_cur[bounce, 1] = swap_halves(packed).astype(BF16)
        rx_cur[bounce, 0] = st_cur[bounce, 0]

    stage_current(0, inc_pack[...])

    slot = lax.broadcasted_iota(jnp.int32, (32, 16), 0)
    there = lax.broadcasted_iota(jnp.int32, (32, 16), 1)
    place = slot // NX
    z_of = lax.rem(z0 + ring_offset(place), NZ)
    match = there == lax.rem(z_of, 4) * NX + lax.rem(x0 + lax.rem(slot, NX), NX)
    own_z = (z_of // 4) == zh0
    pick_own = jnp.where(match & own_z, 1.0, 0.0).astype(BF16)
    pick_far = jnp.where(match & jnp.logical_not(own_z), 1.0, 0.0).astype(BF16)
    a_row = lax.broadcasted_iota(jnp.int32, (128, NOBS), 0)
    a_lane = lax.broadcasted_iota(jnp.int32, (128, NOBS), 1)
    a_of = (
        lax.rem(y0 + ring_offset(a_lane // 128), NY) * 4 + zh0 * 2 + lax.rem(c0 + lax.rem(a_lane // TILE, 2), 2)
    )
    spread = jnp.where(a_row == a_of, 1.0, 0.0).astype(BF16)

    right_t[...] = jnp.zeros((DEPTH, NSRC), F32)
    right_t[18:24, :] = jnp.ones((6, NSRC), F32)
    b_row = lax.broadcasted_iota(jnp.int32, (32, NSRC), 0)
    b_lane = lax.broadcasted_iota(jnp.int32, (32, NSRC), 1)
    right_t[24:56, :] = jnp.where(b_row == b_lane // TILE, 1.0, 0.0)

    pl.semaphore_wait(barrier, len(XZ) + len(YC))

    def send(src, dst, sem, **offset):
        pltpu.make_async_remote_copy(
            src_ref=src, dst_ref=dst, send_sem=send_sem.at[sem], recv_sem=recv_sem.at[sem],
            device_id=device(**offset), device_id_type=MESH,
        ).start()

    def arrived(ref, sem):
        pltpu.make_async_copy(ref, ref, recv_sem.at[sem]).wait()

    def left_here(ref, sem):
        pltpu.make_async_copy(ref, ref, send_sem.at[sem]).wait()

    near_slots, far_slots = NEAR_Z * NX, (NZ - NEAR_Z) * NX
    S_OBS, S_VIS, S_PWN, S_PWF, S_CUR, S_SUM = 0, 1, 2, 3, 4, 10

    def sem_of(base, x, z):
        return base if src_slot(-x, -z) < near_slots else base + 1

    def send_place(near):
        for x, z in XZ:
            if (src_slot(-x, -z) < near_slots) == near:
                send(st_pw.at[x % 2], rx_pw.at[src_slot(-x, -z)], sem_of(S_PWN, x, z), dx=x, dz=z)

    send(st_vis, rx_vis, S_VIS, dz=4)
    for y, c in YC:
        send(st_obs.at[c], rx_obs.at[obs_slot(-y, c)], S_OBS, dy=y, dc=c)
    send_place(True)
    send_place(False)

    def send_current(bounce):
        for x, z in XZ:
            send(
                st_cur.at[bounce, x % 2], rx_cur.at[bounce, src_slot(-x, -z)],
                sem_of(S_CUR + 2 * bounce, x, z), dx=x, dz=z,
            )

    send_current(0)

    arrived(rx_obs.at[pl.ds(1, NY * NC - 1)], S_OBS)
    for y in range(NY):
        obs_all[:, y * 128 : (y + 1) * 128] = rx_obs[2 * y] + rx_obs[2 * y + 1]
    big_pos = 8.0 * obs_all[0:3, :]
    h, m, l = split3(big_pos)
    for i, part in enumerate((h, m, l, h, m, h)):
        left_f[3 * i : 3 * i + 3, :] = part
    left_f[18:21, :] = jnp.ones((3, NOBS), F32)
    norms = split3(jnp.sum(big_pos * big_pos, axis=0, keepdims=True) + 64.0 * 0.0025)
    for i, part in enumerate(norms):
        left_f[21 + i : 22 + i, :] = part
    left_f[56:64, :] = jnp.zeros((8, NOBS), F32)

    def source_side(first, count):
        groups = range(first // 128, (first + count) // 128)
        for g in groups:
            pw_all[:, g * 128 : (g + 1) * 128] = rx_pw[2 * g] + rx_pw[2 * g + 1]
        span = slice(first, first + count)
        big_src = 8.0 * pw_all[0:3, span]
        h, m, l = split3(big_src)
        for i, part in enumerate((h, h, h, m, m, l)):
            right_t[3 * i : 3 * i + 3, span] = -2.0 * part
        norms = split3(jnp.sum(big_src * big_src, axis=0, keepdims=True))
        for i, part in enumerate(norms):
            right_t[18 + i : 19 + i, span] = part
        for g in groups:
            right[g * 128 : (g + 1) * 128, :] = jnp.transpose(right_t[:, g * 128 : (g + 1) * 128]).astype(BF16)

    arrived(rx_pw.at[pl.ds(1, near_slots - 1)], S_PWN)
    source_side(0, NEAR)
    arrived(rx_vis, S_VIS)
    seen = jnp.dot(pick_own, st_vis[...], preferred_element_type=F32) + jnp.dot(
        pick_far, rx_vis[...], preferred_element_type=F32
    )
    seen_all = jnp.dot(seen.astype(BF16), spread, preferred_element_type=F32)
    left_f[24:56, :] = BIG * (1.0 - seen_all)
    left[...] = left_f[...].astype(BF16)

    def operand(bounce, groups, first, x_ref):
        span = len(groups) * 128
        for g in groups:
            lanes = slice(g * 128, (g + 1) * 128)
            even, odd = rx_cur[bounce, 2 * g].astype(F32), rx_cur[bounce, 2 * g + 1].astype(F32)
            same = jnp.where(low, even, odd)
            s = (same, pltpu.roll(same, 4, axis=0), swap_halves(jnp.where(low, odd, even)))
            p = [pw_all[k : k + 1, lanes] for k in range(3)]
            w = pw_all[3:4, lanes]
            rows = []
            turned = []
            for k in range(3):
                i, j = (k + 1) % 3, (k + 2) % 3
                cross = p[i] * s[j] - p[j] * s[i]
                both = jnp.where(top, s[k], pltpu.roll(cross, 4, axis=0)) * w
                rows.append(both)
                turned.append(
                    jnp.where(lax.rem(sub, 4) < 2, -pltpu.roll(both, 6, axis=0), pltpu.roll(both, 2, axis=0))
                )
            at = (g - first) * 128
            for begin, parts in ((at, rows), (span + at, turned)):
                exact = jnp.concatenate(parts, axis=0)
                high = exact.astype(BF16)
                rest = (exact - high.astype(F32)).astype(BF16)
                x_ref[:, begin : begin + 128] = jnp.concatenate([high, rest], axis=0)

    near_groups = range(0, NEAR // 128)
    far_groups = range(NEAR // 128, NSRC // 128)

    def near_operand(bounce):
        arrived(rx_cur.at[bounce, pl.ds(1, near_slots - 1)], S_CUR + 2 * bounce)
        operand(bounce, near_groups, 0, x_near)

    def far_operand(bounce):
        arrived(rx_cur.at[bounce, pl.ds(near_slots, far_slots)], S_CUR + 2 * bounce + 1)
        operand(bounce, far_groups, NEAR // 128, x_far)

    def near_product(lanes):
        both = jnp.dot(x_near[...], k_all[0 : 2 * NEAR, lanes], preferred_element_type=F32)
        return both[0 : ROWS // 2] + both[ROWS // 2 : ROWS]

    def far_product(lanes):
        both = jnp.dot(x_far[...], k_all[2 * NEAR : 2 * NSRC, lanes], preferred_element_type=F32)
        return both[0 : ROWS // 2] + both[ROWS // 2 : ROWS]

    def messages(bounce, place, total):
        lanes = slice(place * 128, (place + 1) * 128)
        y = RING_ORDER[place]
        p = [obs_all[k : k + 1, lanes] for k in range(3)]
        n = [obs_all[3 + k : 4 + k, lanes] for k in range(3)]
        a = [total[8 * k : 8 * k + 8, :] for k in range(3)]
        d = [
            p[(k + 1) % 3] * a[(k + 2) % 3] - p[(k + 2) % 3] * a[(k + 1) % 3] - pltpu.roll(a[k], 4, axis=0)
            for k in range(3)
        ]
        s = [n[(k + 1) % 3] * d[(k + 2) % 3] - n[(k + 2) % 3] * d[(k + 1) % 3] for k in range(3)]
        pair = jnp.where(top, s[0], pltpu.roll(s[1], 4, axis=0))
        for c, packed in (
            (0, jnp.where(low, pair, swap_halves(s[2]))),
            (1, jnp.where(low, swap_halves(pair), s[2])),
        ):
            if place == 0 and c == 0:
                rx_sum[bounce, 0] = packed.astype(BF16)
            else:
                st_sum[bounce, 2 * place + c] = packed.astype(BF16)
                send(
                    st_sum.at[bounce, 2 * place + c], rx_sum.at[bounce, obs_slot(-y, c)],
                    S_SUM + bounce, dy=y, dc=c,
                )

    def squares(block, lanes, ref):
        rows = pl.ds(aligned(block * BLOCK, BLOCK), BLOCK)
        ref[:, 0 : lanes.size] = jnp.dot(right[rows, :], left[:, lanes], preferred_element_type=F32)

    def fill(ref, block, lanes):
        near = block < NEAR // BLOCK
        re_row = aligned(block * BLOCK + either(near, 0, NEAR), BLOCK)
        im_row = aligned(block * BLOCK + either(near, NEAR, NSRC), BLOCK)
        for r in range(0, BLOCK, 16):
            for v in range(0, lanes.size, 256):
                re, im = pair_kernel(ref[r : r + 16, v : v + 256])
                at = pl.ds(aligned(lanes.start + v, BLOCK), BLOCK)
                k_all[pl.ds(re_row + r, 16), at] = re
                k_all[pl.ds(im_row + r, 16), at] = im

    def sweep(unit, count, last):
        squares(*unit(0), s_a)

        def two(i, _):
            squares(*unit(2 * i + 1), s_b)
            fill(s_a, *unit(2 * i))
            squares(*unit(jnp.minimum(2 * i + 2, last)), s_a)
            fill(s_b, *unit(2 * i + 1))
            return 0

        lax.fori_loop(0, count // 2, two, 0)

    near_blocks, far_blocks = NEAR // BLOCK, FAR // BLOCK
    sweep(
        lambda k: (k // 2, pl.ds(pl.multiple_of(lax.rem(k, 2) * HALF, HALF), HALF)),
        2 * near_blocks, 2 * near_blocks - 1,
    )
    near_operand(0)
    arrived(rx_pw.at[pl.ds(near_slots, far_slots)], S_PWF)
    source_side(NEAR, FAR)
    far_operand(0)

    def finish(bounce, q):
        lanes = slice(q * BLOCK, (q + 1) * BLOCK)
        total = acc[:, lanes] + far_product(lanes)
        for place in (2 * q + 1, 2 * q):
            messages(bounce, place, total[:, (place % 2) * 128 : (place % 2) * 128 + 128])

    for h in (1, 0):
        units = [
            (near_blocks + b, pl.ds(h * HALF + q * BLOCK, BLOCK)) for q in (1, 0) for b in range(far_blocks)
        ]
        stages = (s_a, s_b)
        squares(*units[0], s_a)
        for k, unit in enumerate(units):
            if k + 1 < len(units):
                squares(*units[k + 1], stages[(k + 1) % 2])
            if k % far_blocks == 0:
                q = 2 * h + 1 - k // far_blocks
                acc[:, q * BLOCK : (q + 1) * BLOCK] = near_product(slice(q * BLOCK, (q + 1) * BLOCK))
            fill(stages[k % 2], *unit)
            if k % far_blocks == far_blocks - 1:
                finish(0, 2 * h + 1 - k // far_blocks)

    current = None
    for bounce in range(ITERS):
        if bounce > 0:
            near_operand(bounce)
            for h in (1, 0):
                acc[:, h * HALF : (h + 1) * HALF] = near_product(slice(h * HALF, (h + 1) * HALF))
            far_operand(bounce)
            for q in (3, 2, 1, 0):
                finish(bounce, q)
        arrived(rx_sum.at[bounce, pl.ds(1, NY * NC - 1)], S_SUM + bounce)
        current = inc_pack[...] + jnp.sum(rx_sum[bounce].astype(F32), axis=0)
        if bounce + 1 < ITERS:
            stage_current(bounce + 1, current)
            send_current(bounce + 1)

    third = swap_halves(current)
    for part in range(2):
        for k in range(2):
            out_ref[part, k] = current[4 * k + 2 * part : 4 * k + 2 * part + 2, 0:TILE]
        out_ref[part, 2] = third[2 * part : 2 * part + 2, 0:TILE]

    left_here(rx_obs.at[pl.ds(1, NY * NC - 1)], S_OBS)
    left_here(rx_vis, S_VIS)
    left_here(rx_pw.at[pl.ds(1, near_slots - 1)], S_PWN)
    left_here(rx_pw.at[pl.ds(near_slots, far_slots)], S_PWF)
    for bounce in range(ITERS):
        left_here(rx_cur.at[bounce, pl.ds(1, near_slots - 1)], S_CUR + 2 * bounce)
        left_here(rx_cur.at[bounce, pl.ds(near_slots, far_slots)], S_CUR + 2 * bounce + 1)
        left_here(rx_sum.at[bounce, pl.ds(1, NY * NC - 1)], S_SUM + bounce)


def shards(positions, orient, areas, incident, visible):
    vmem = pltpu.VMEM
    scratch = [
        vmem((3, TILE), F32), vmem((2, TILE), F32), vmem((1, TILE), F32), vmem(incident.shape, F32),
        vmem((16, 1, 32), jnp.int32),
        vmem((2, 8, 128), F32), vmem((16, 8, 128), F32),
        vmem((2, 4, 128), F32), vmem((32, 4, 128), F32),
        vmem((16, 128), BF16), vmem((16, 128), BF16),
        vmem((ITERS, 2, 8, 128), BF16), vmem((ITERS, 32, 8, 128), BF16),
        vmem((ITERS, 16, 8, 128), BF16), vmem((ITERS, 16, 8, 128), BF16),
        vmem((8, 128), F32), vmem((8, NOBS), F32), vmem((4, NSRC), F32),
        vmem((DEPTH, NSRC), F32), vmem((NSRC, DEPTH), BF16), vmem((DEPTH, NOBS), F32), vmem((DEPTH, NOBS), BF16),
        vmem((BLOCK, HALF), F32), vmem((BLOCK, HALF), F32),
        vmem((2 * NSRC, NOBS), BF16),
        vmem((ROWS, 2 * NEAR), BF16), vmem((ROWS, 2 * FAR), BF16), vmem((ROWS // 2, NOBS), F32),
        pltpu.SemaphoreType.DMA((5,)), pltpu.SemaphoreType.DMA((13,)), pltpu.SemaphoreType.DMA((13,)),
    ]
    return pl.pallas_call(
        body,
        out_shape=jax.ShapeDtypeStruct(incident.shape, F32),
        in_specs=[pl.BlockSpec(memory_space=pl.ANY)] * 5,
        out_specs=pl.BlockSpec(memory_space=vmem),
        scratch_shapes=scratch,
        compiler_params=pltpu.CompilerParams(
            collective_id=0, has_side_effects=True, vmem_limit_bytes=60 * 2**20
        ),
        cost_estimate=pl.CostEstimate(flops=3_000_000_000, bytes_accessed=1_000_000, transcendentals=4_000_000),
    )(positions, orient, areas.reshape(1, -1), incident, jnp.transpose(visible, (1, 2, 0)))


def solution(mesh):
    in_specs = (
        P(None, ("row", "col")),
        P(None, ("row", "col")),
        P(("row", "col")),
        P(None, None, None, ("row", "col")),
        P("row", None, "col"),
    )
    out_specs = P(None, None, None, ("row", "col"))
    return jax.shard_map(shards, mesh=mesh, in_specs=in_specs, out_specs=out_specs, check_vma=False)
```

time: 66.6 us -> 59 us (0.89)
  Pallas kernels: 63.7 us -> 57.5 us
  local copies, waits for them, and re-layouts: 2.68 us -> 1.29 us
    pallas_call x1, Pallas kernels: 63.7 us -> 57.5 us  [shards(): pl.pallas_call(body, out_shape=jax.ShapeDtypeStruct(incident.shape, F32),...]
    unnamed x11 -> x1, local copies, waits for them, and re-layouts: 2.68 us -> 1.29 us
where the time goes in v2:
time: 59 us; the launch traced here: 58.8 us
  Pallas kernels  57.5 us (97%)
  local copies, waits for them, and re-layouts  1.29 us (2%)
    pallas_call x1, Pallas kernels, shards(): pl.pallas_call(body, out_shape=jax.ShapeDtypeStruct(incident.shape, F32),...  57.5 us
    unnamed x1, local copies, waits for them, and re-layouts  1.29 us

profile of v2, /device:TPU:1, one launch (start us, length us, event | category | flops | bytes accessed | tf_op | source)
XLA Modules:
  0.0 58.8 jit_solution(855618838392785605)
XLA Ops:
  0.0 57.5 %shard_map.55 = f32[2,3,2,64]{3,2,1,0:T(2,128)} custom-call(f32[3,64]{1,0:T(4,128)} %pos_hbm.1, f32[2,64]{1,0:T(2,128)} %ori_hbm.1, f32[1,64]{1,0:T(1,128)} %bitcast.3, f32[2,3,2,64]{3,2,1,0:T(2,128)} %inc_hbm.1, s32[16,1,32]{2,1,0:T(1,128)} %bitcast.2), custom_call_target="tpu_custom_call" | custom-call | flops 3000000000 | bytes 1000000 | tf_op jit(solution)/shard_map/pallas_call | solution.py:432
  57.5 1.3 %copy.7 = f32[2,3,2,64]{3,2,1,0:T(2,128)} copy(f32[2,3,2,64]{3,2,1,0:T(2,128)} %shard_map.55) | data formatting | bytes 6144

commit v3 on v2

--- a/solution.py
+++ b/solution.py
@@ -194,16 +194,21 @@
     def sem_of(base, x, z):
         return base if src_slot(-x, -z) < near_slots else base + 1
 
-    def send_place(near):
-        for x, z in XZ:
-            if (src_slot(-x, -z) < near_slots) == near:
-                send(st_pw.at[x % 2], rx_pw.at[src_slot(-x, -z)], sem_of(S_PWN, x, z), dx=x, dz=z)
+    def send_place(x, z):
+        send(st_pw.at[x % 2], rx_pw.at[src_slot(-x, -z)], sem_of(S_PWN, x, z), dx=x, dz=z)
+
+    near_peers = [(x, z) for x, z in XZ if src_slot(-x, -z) < near_slots]
+    far_peers = [(x, z) for x, z in XZ if src_slot(-x, -z) >= near_slots]
 
     send(st_vis, rx_vis, S_VIS, dz=4)
-    for y, c in YC:
-        send(st_obs.at[c], rx_obs.at[obs_slot(-y, c)], S_OBS, dy=y, dc=c)
-    send_place(True)
-    send_place(False)
+    for i in range(max(len(YC), len(near_peers))):
+        if i < len(YC):
+            y, c = YC[i]
+            send(st_obs.at[c], rx_obs.at[obs_slot(-y, c)], S_OBS, dy=y, dc=c)
+        if i < len(near_peers):
+            send_place(*near_peers[i])
+    for x, z in far_peers:
+        send_place(x, z)
 
     def send_current(bounce):
         for x, z in XZ:
@@ -310,8 +315,8 @@
         s = [n[(k + 1) % 3] * d[(k + 2) % 3] - n[(k + 2) % 3] * d[(k + 1) % 3] for k in range(3)]
         pair = jnp.where(top, s[0], pltpu.roll(s[1], 4, axis=0))
         for c, packed in (
+            (1, jnp.where(low, swap_halves(pair), s[2])),
             (0, jnp.where(low, pair, swap_halves(s[2]))),
-            (1, jnp.where(low, swap_halves(pair), s[2])),
         ):
             if place == 0 and c == 0:
                 rx_sum[bounce, 0] = packed.astype(BF16)
@@ -352,12 +357,17 @@
     near_blocks, far_blocks = NEAR // BLOCK, FAR // BLOCK
     sweep(
         lambda k: (k // 2, pl.ds(pl.multiple_of(lax.rem(k, 2) * HALF, HALF), HALF)),
-        2 * near_blocks, 2 * near_blocks - 1,
+        2 * near_blocks - 2, 2 * near_blocks - 3,
     )
     near_operand(0)
+    last_near = [(near_blocks - 1, pl.ds(h * HALF, HALF)) for h in (0, 1)]
+    squares(*last_near[0], s_a)
+    squares(*last_near[1], s_b)
     arrived(rx_pw.at[pl.ds(near_slots, far_slots)], S_PWF)
     source_side(NEAR, FAR)
+    fill(s_a, *last_near[0])
     far_operand(0)
+    fill(s_b, *last_near[1])
 
     def finish(bounce, q):
         lanes = slice(q * BLOCK, (q + 1) * BLOCK)
@@ -381,6 +391,17 @@
             if k % far_blocks == far_blocks - 1:
                 finish(0, 2 * h + 1 - k // far_blocks)
 
+    def sent_earlier():
+        left_here(rx_obs.at[pl.ds(1, NY * NC - 1)], S_OBS)
+        left_here(rx_vis, S_VIS)
+        left_here(rx_pw.at[pl.ds(1, near_slots - 1)], S_PWN)
+        left_here(rx_pw.at[pl.ds(near_slots, far_slots)], S_PWF)
+        for bounce in range(ITERS):
+            left_here(rx_cur.at[bounce, pl.ds(1, near_slots - 1)], S_CUR + 2 * bounce)
+            left_here(rx_cur.at[bounce, pl.ds(near_slots, far_slots)], S_CUR + 2 * bounce + 1)
+            if bounce < ITERS - 1:
+                left_here(rx_sum.at[bounce, pl.ds(1, NY * NC - 1)], S_SUM + bounce)
+
     current = None
     for bounce in range(ITERS):
         if bounce > 0:
@@ -390,6 +411,8 @@
             far_operand(bounce)
             for q in (3, 2, 1, 0):
                 finish(bounce, q)
+        if bounce == ITERS - 1:
+            sent_earlier()
         arrived(rx_sum.at[bounce, pl.ds(1, NY * NC - 1)], S_SUM + bounce)
         current = inc_pack[...] + jnp.sum(rx_sum[bounce].astype(F32), axis=0)
         if bounce + 1 < ITERS:
@@ -401,15 +424,7 @@
         for k in range(2):
             out_ref[part, k] = current[4 * k + 2 * part : 4 * k + 2 * part + 2, 0:TILE]
         out_ref[part, 2] = third[2 * part : 2 * part + 2, 0:TILE]
-
-    left_here(rx_obs.at[pl.ds(1, NY * NC - 1)], S_OBS)
-    left_here(rx_vis, S_VIS)
-    left_here(rx_pw.at[pl.ds(1, near_slots - 1)], S_PWN)
-    left_here(rx_pw.at[pl.ds(near_slots, far_slots)], S_PWF)
-    for bounce in range(ITERS):
-        left_here(rx_cur.at[bounce, pl.ds(1, near_slots - 1)], S_CUR + 2 * bounce)
-        left_here(rx_cur.at[bounce, pl.ds(near_slots, far_slots)], S_CUR + 2 * bounce + 1)
-        left_here(rx_sum.at[bounce, pl.ds(1, NY * NC - 1)], S_SUM + bounce)
+    left_here(rx_sum.at[ITERS - 1, pl.ds(1, NY * NC - 1)], S_SUM + ITERS - 1)
 
 
 def shards(positions, orient, areas, incident, visible):

time: 59 us -> 58.9 us (level)
  no operation moved by 1% of the time
where the time goes in v3:
time: 58.9 us; the launch traced here: 58.6 us
  Pallas kernels  57.3 us (97%)
  local copies, waits for them, and re-layouts  1.29 us (2%)
    pallas_call x1, Pallas kernels, shards(): pl.pallas_call(body, out_shape=jax.ShapeDtypeStruct(incident.shape, F32),...  57.3 us
    unnamed x1, local copies, waits for them, and re-layouts  1.29 us

profile of v3, /device:TPU:1, one launch (start us, length us, event | category | flops | bytes accessed | tf_op | source)
XLA Modules:
  0.0 58.6 jit_solution(7204140510940550796)
XLA Ops:
  0.0 57.3 %shard_map.55 = f32[2,3,2,64]{3,2,1,0:T(2,128)} custom-call(f32[3,64]{1,0:T(4,128)} %pos_hbm.1, f32[2,64]{1,0:T(2,128)} %ori_hbm.1, f32[1,64]{1,0:T(1,128)} %bitcast.3, f32[2,3,2,64]{3,2,1,0:T(2,128)} %inc_hbm.1, s32[16,1,32]{2,1,0:T(1,128)} %bitcast.2), custom_call_target="tpu_custom_call" | custom-call | flops 3000000000 | bytes 1000000 | tf_op jit(solution)/shard_map/pallas_call | solution.py:447
  57.4 1.3 %copy.7 = f32[2,3,2,64]{3,2,1,0:T(2,128)} copy(f32[2,3,2,64]{3,2,1,0:T(2,128)} %shard_map.55) | data formatting | bytes 6144
